TPU v7x, 32 devices: a whole 2x2x4 slice. The times are simulated.
32 devices in a mesh: dp: 1, ctx: 16 (over z, x, core), tp: 2 (over y).
Axes of the slice: x: 2, y: 2, z: 4, core: 2. Of those that a mesh axis runs over, the one named last changes fastest.
Arguments:
- query: bfloat16 [1, 2048, 8192], P('dp', 'ctx', 'tp'), may hold values from -80 to 80
- key: bfloat16 [1, 2048, 1024], P('dp', 'ctx', 'tp'), may hold values from -6 to 6
- value: bfloat16 [1, 2048, 1024], P('dp', 'ctx', 'tp'), may hold values from -6 to 6
- key_shift: float32 [1, 2048, 1024], P('dp', 'ctx', 'tp'), may hold values from -0.6 to 0.6
- value_shift: float32 [1, 2048, 1024], P('dp', 'ctx', 'tp'), may hold values from -0.6 to 0.6
- doc_ids: int32 [1, 2048], P('dp', 'ctx'), may hold values from 0 to 31, never falling along the last dimension, each value on 1 to 512 neighbouring positions
- target: bfloat16 [1, 2048, 8192], P('dp', 'ctx', 'tp'), may hold values from -160 to 160
Outputs:
- attn: bfloat16 [1, 2048, 8192], P('dp', 'ctx', 'tp')
- new_key_shift: float32 [1, 2048, 1024], P('dp', 'ctx', 'tp')
- new_value_shift: float32 [1, 2048, 1024], P('dp', 'ctx', 'tp')
All inputs are finite; a program needn't handle non-finite values.
Results may differ from a plain program's by a relative error of at most 0.005.
Values may be sent and summed in bfloat16 or wider, within the bound.
A program may use at most 128 MiB of HBM per device.

v0:
```python
import math

import jax
import jax.numpy as jnp
from jax import lax
from jax.sharding import PartitionSpec as P

HEADS = 64
KV_HEADS = 8
HEAD = 128


step_size = 0.1
radius_scale = 0.13


def passed_along(block, axis, distance):
    devices = range(lax.axis_size(axis))
    route = [(i - distance, i) for i in devices if i - distance in devices]
    return lax.ppermute(block, axis, route)


def for_sending(value):
    return jax.tree.map(lambda a: a.astype(jnp.bfloat16) if a.dtype == jnp.float32 else a, value)


def per_device(query, key, value, key_shift, value_shift, doc_ids, target):
    tokens = query.shape[1]
    kv_local = key.shape[2] // HEAD
    group = HEADS // KV_HEADS
    half = group // 2
    scale = 1.0 / math.sqrt(HEAD)
    ctx_count = lax.axis_size("ctx")
    seq_total = tokens * ctx_count
    doc_limit = min(2048, seq_total // 4)
    reach = (doc_limit + tokens - 2) // tokens
    width = (reach + 1) * tokens
    where_ctx = lax.axis_index("ctx")
    key_new = (key[0].astype(jnp.float32) + key_shift[0]).astype(jnp.bfloat16)
    val_new = (value[0].astype(jnp.float32) + value_shift[0]).astype(jnp.bfloat16)
    own_docs = doc_ids[0]
    local = (key_new, val_new, own_docs)
    pieces = [local]
    current = local
    for offset in range(reach):
        current = passed_along((current[0], current[1], current[2]), "ctx", 1)
        pieces.append(current)
    ordered = pieces[::-1]
    window_keys = jnp.concatenate([piece[0] for piece in ordered], 0)
    window_vals = jnp.concatenate([piece[1] for piece in ordered], 0)
    window_docs = jnp.concatenate([piece[2] for piece in ordered], 0)
    first = (where_ctx - reach) * tokens
    key_pos = first + jnp.arange(width, dtype=jnp.int32)
    query_pos = where_ctx * tokens + jnp.arange(tokens, dtype=jnp.int32)
    allowed = (
        (window_docs[None, :] == own_docs[:, None])
        & (key_pos[None, :] <= query_pos[:, None])
        & (key_pos[None, :] >= 0)
    )
    q_items = jnp.transpose(
        query[0].reshape(tokens, kv_local, 2, half, HEAD), (1, 2, 0, 3, 4)
    ).reshape(kv_local * 2, tokens, half, HEAD)
    t_items = jnp.transpose(
        target[0].reshape(tokens, kv_local, 2, half, HEAD), (1, 2, 0, 3, 4)
    ).reshape(kv_local * 2, tokens, half, HEAD)
    k_items = jnp.repeat(
        jnp.transpose(window_keys.reshape(width, kv_local, HEAD), (1, 0, 2)), 2, axis=0
    )
    v_items = jnp.repeat(
        jnp.transpose(window_vals.reshape(width, kv_local, HEAD), (1, 0, 2)), 2, axis=0
    )

    def per_item(items):
        q_item, t_item, k_item, v_item = items
        scores = (
            jnp.einsum("thd,wd->htw", q_item, k_item, preferred_element_type=jnp.float32) * scale
        )
        scores = jnp.where(allowed[None], scores, -jnp.inf)
        top = jnp.max(scores, -1, keepdims=True)
        expo = jnp.exp(scores - top)
        total = jnp.sum(expo, -1, keepdims=True)
        expo16 = expo.astype(jnp.bfloat16)
        out = jnp.einsum("htw,wd->htd", expo16, v_item, preferred_element_type=jnp.float32) / total
        dprob = jnp.einsum("thd,wd->htw", t_item, v_item, preferred_element_type=jnp.float32)
        delta = jnp.sum(
            jnp.transpose(t_item, (1, 0, 2)).astype(jnp.float32) * out, -1, keepdims=True
        )
        prob = expo / total
        ds16 = (prob * (dprob - delta)).astype(jnp.bfloat16)
        prob16 = prob.astype(jnp.bfloat16)
        dk = jnp.einsum("htw,thd->wd", ds16, q_item, preferred_element_type=jnp.float32) * scale
        dv = jnp.einsum("htw,thd->wd", prob16, t_item, preferred_element_type=jnp.float32)
        return (out.astype(jnp.bfloat16), dk, dv)

    out_items, dk_items, dv_items = lax.map(per_item, (q_items, t_items, k_items, v_items))
    attn = jnp.transpose(
        out_items.reshape(kv_local, 2, half, tokens, HEAD), (3, 0, 1, 2, 4)
    ).reshape(1, tokens, kv_local * group * HEAD)
    dk_heads = jnp.sum(dk_items.reshape(kv_local, 2, width, HEAD), 1)
    dv_heads = jnp.sum(dv_items.reshape(kv_local, 2, width, HEAD), 1)
    grad_window_k = jnp.transpose(dk_heads, (1, 0, 2)).reshape(reach + 1, tokens, kv_local * HEAD)
    grad_window_v = jnp.transpose(dv_heads, (1, 0, 2)).reshape(reach + 1, tokens, kv_local * HEAD)
    carried = (grad_window_k[0], grad_window_v[0])
    for index in range(1, reach + 1):
        moved = passed_along((for_sending(carried[0]), for_sending(carried[1])), "ctx", -1)
        carried = (moved[0] + grad_window_k[index], moved[1] + grad_window_v[index])
    grad_key, grad_val = carried
    local_sq = jnp.sum(grad_key * grad_key) + jnp.sum(grad_val * grad_val)
    overall = lax.psum(local_sq, ("dp", "ctx", "tp"))
    count = lax.axis_size("dp") * seq_total * 2 * KV_HEADS * HEAD
    rms = jnp.sqrt(overall / count + 1e-05)
    moved_key = key_shift[0] + step_size / rms * grad_key
    moved_val = value_shift[0] + step_size / rms * grad_val
    part_sq = jnp.sum(moved_key * moved_key, -1) + jnp.sum(moved_val * moved_val, -1)
    size_sq = lax.psum(part_sq, "tp")
    radius = radius_scale * math.sqrt(2 * KV_HEADS * HEAD)
    factor = jnp.minimum(1.0, radius / jnp.sqrt(size_sq + 1e-06))[:, None]
    return (attn, (moved_key * factor)[None], (moved_val * factor)[None])


def solution(mesh):
    in_specs = (
        P("dp", "ctx", "tp"),
        P("dp", "ctx", "tp"),
        P("dp", "ctx", "tp"),
        P("dp", "ctx", "tp"),
        P("dp", "ctx", "tp"),
        P("dp", "ctx"),
        P("dp", "ctx", "tp"),
    )
    out_specs = (P("dp", "ctx", "tp"), P("dp", "ctx", "tp"), P("dp", "ctx", "tp"))
    return jax.shard_map(
        per_device, mesh=mesh, in_specs=in_specs, out_specs=out_specs, check_vma=False
    )
```

profile of v0, /device:TPU:0, one launch (start us, length us, event | category | flops | bytes accessed | tf_op | source)
XLA Modules:
  0.0 215.7 jit_solution(10451153786582271256)
XLA Ops:
  0.7 2.5 %collective-permute-start = (s32[128]{0:T(128)}, s32[128]{0:T(128)S(1)}, u32[]{:S(2)}, u32[]{:S(2)}) collective-permute-start(s32[128]{0:T(128)} %bitcast.212), channel_id=1, source_target_pairs={{0,2},{2,4},{4,6},{6,8},{8,10},{10,12},{12,14},{14,16},{16,18},{18... | collective-permute-start | bytes 1544 | tf_op jit(solution)/shard_map/ppermute | solution.py:20
  5.3 4.5 %collective-permute-start.4 = (bf16[128,512]{0,1:T(8,128)(2,1)S(1)}, bf16[128,512]{0,1:T(8,128)(2,1)S(1)}, u32[]{:S(2)}, u32[]{:S(2)}) collective-permute-start(bf16[128,512]{0,1:T(8,128)(2,1)S(1)} %fusion.47), channel_id=1, source_target_pairs={{0,2},{2,4},{4,6},{6,8},{8,10},{10,12},{12,14},{14,16},{16,18},{18... | collective-permute-start | bytes 393224 | tf_op jit(solution)/shard_map/ppermute | solution.py:20
  12.1 3.6 %collective-permute-start.1 = (s32[128]{0:T(128)S(1)}, s32[128]{0:T(128)S(1)}, u32[]{:S(2)}, u32[]{:S(2)}) collective-permute-start(s32[128]{0:T(128)S(1)} %collective-permute-done), channel_id=1, source_target_pairs={{0,2},{2,4},{4,6},{6,8},{8,10},{10,12},{12,14},{14,16},{16,18},{18... | collective-permute-start | bytes 1544 | tf_op jit(solution)/shard_map/ppermute | solution.py:20
  16.5 2.2 %collective-permute-start.2 = (s32[128]{0:T(128)S(1)}, s32[128]{0:T(128)S(1)}, u32[]{:S(2)}, u32[]{:S(2)}) collective-permute-start(s32[128]{0:T(128)S(1)} %collective-permute-done.1), channel_id=1, source_target_pairs={{0,2},{2,4},{4,6},{6,8},{8,10},{10,12},{12,14},{14,16},{16,18},{18... | collective-permute-start | bytes 1544 | tf_op jit(solution)/shard_map/ppermute | solution.py:20
  19.5 3.7 %collective-permute-start.3 = (s32[128]{0:T(128)S(1)}, s32[128]{0:T(128)S(1)}, u32[]{:S(2)}, u32[]{:S(2)}) collective-permute-start(s32[128]{0:T(128)S(1)} %collective-permute-done.2), channel_id=1, source_target_pairs={{0,2},{2,4},{4,6},{6,8},{8,10},{10,12},{12,14},{14,16},{16,18},{18... | collective-permute-start | bytes 1544 | tf_op jit(solution)/shard_map/ppermute | solution.py:20
  26.7 4.1 %collective-permute-start.9 = (bf16[128,512]{0,1:T(8,128)(2,1)S(1)}, bf16[128,512]{0,1:T(8,128)(2,1)S(1)}, u32[]{:S(2)}, u32[]{:S(2)}) collective-permute-start(bf16[128,512]{0,1:T(8,128)(2,1)S(1)} %collective-permute-done.8), channel_id=1, source_target_pairs={{0,2},{2,4},{4,6},{6,8},{8,10},{10,12},{12,14},{14,16},{16,18},{18... | collective-permute-start | bytes 393224 | tf_op jit(solution)/shard_map/ppermute | solution.py:20
  30.9 2.2 %collective-permute-start.5 = (bf16[128,512]{0,1:T(8,128)(2,1)S(1)}, bf16[128,512]{0,1:T(8,128)(2,1)S(1)}, u32[]{:S(2)}, u32[]{:S(2)}) collective-permute-start(bf16[128,512]{0,1:T(8,128)(2,1)S(1)} %collective-permute-done.4), channel_id=1, source_target_pairs={{0,2},{2,4},{4,6},{6,8},{8,10},{10,12},{12,14},{14,16},{16,18},{18... | collective-permute-start | bytes 393224 | tf_op jit(solution)/shard_map/ppermute | solution.py:20
  33.1 5.1 %collective-permute-start.10 = (bf16[128,512]{0,1:T(8,128)(2,1)S(1)}, bf16[128,512]{0,1:T(8,128)(2,1)S(1)}, u32[]{:S(2)}, u32[]{:S(2)}) collective-permute-start(bf16[128,512]{0,1:T(8,128)(2,1)S(1)} %collective-permute-done.9), channel_id=1, source_target_pairs={{0,2},{2,4},{4,6},{6,8},{8,10},{10,12},{12,14},{14,16},{16,18},{18... | collective-permute-start | bytes 393224 | tf_op jit(solution)/shard_map/ppermute | solution.py:20
  40.1 4.3 %collective-permute-start.11 = (bf16[128,512]{0,1:T(8,128)(2,1)S(1)}, bf16[128,512]{0,1:T(8,128)(2,1)S(1)}, u32[]{:S(2)}, u32[]{:S(2)}) collective-permute-start(bf16[128,512]{0,1:T(8,128)(2,1)S(1)} %collective-permute-done.10), channel_id=1, source_target_pairs={{0,2},{2,4},{4,6},{6,8},{8,10},{10,12},{12,14},{14,16},{16,18},{18... | collective-permute-start | bytes 393224 | tf_op jit(solution)/shard_map/ppermute | solution.py:20
  44.5 2.8 %collective-permute-start.7 = (bf16[128,512]{0,1:T(8,128)(2,1)S(1)}, bf16[128,512]{0,1:T(8,128)(2,1)S(1)}, u32[]{:S(2)}, u32[]{:S(2)}) collective-permute-start(bf16[128,512]{0,1:T(8,128)(2,1)S(1)} %collective-permute-done.6), channel_id=1, source_target_pairs={{0,2},{2,4},{4,6},{6,8},{8,10},{10,12},{12,14},{14,16},{16,18},{18... | collective-permute-start | bytes 393224 | tf_op jit(solution)/shard_map/ppermute | solution.py:20
  50.3 72.4 %while.15 = (s32[]{:T(128)}, bf16[8,4,128,128]{2,3,1,0:T(8,128)(2,1)}, f32[8,640,128]{2,1,0:T(8,128)}, f32[8,640,128]{2,1,0:T(8,128)}, bf16[8,640,128]{2,1,0:T(8...) while((s32[]{:T(128)}, ...), condition=%wide.region_4.5_spmd.clone, body=%wide.region_0.4_spmd.clone.sunk | while | flops 425081344 | bytes 9209617 | solution.py:95
  55.0 2.4 %fusion.75 = f32[8,640,128]{2,1,0:T(8,128)} fusion(f32[8,640,128]{2,1,0:T(8,128)} %get-tuple-element.236, s32[]{:T(128)S(6)} %copy.74, f32[4,128]{1,0:T(4,128)S(1)} %fusion.74, f32[4,128,640]{1,2,0:T(8,128)S(1)} %get-tuple-element.216, f32[4,128]{1,0:T(4,128)S(1)} %fusion.73, f32[4,128]{1,0:T(4,128)S(1)} %get-tuple-element.217, ...), kind=kOutput, calls=%fused_computation.16.clone.1 | convolution fusion | flops 169492480 | bytes 2072576 | tf_op jit(solution)/shard_map/while/body/eval_jaxpr/htw,thd->wd/dot_general | solution.py:91
  64.1 2.4 %fusion.75 = f32[8,640,128]{2,1,0:T(8,128)} fusion(f32[8,640,128]{2,1,0:T(8,128)} %get-tuple-element.236, s32[]{:T(128)S(6)} %copy.74, f32[4,128]{1,0:T(4,128)S(1)} %fusion.74, f32[4,128,640]{1,2,0:T(8,128)S(1)} %get-tuple-element.216, f32[4,128]{1,0:T(4,128)S(1)} %fusion.73, f32[4,128]{1,0:T(4,128)S(1)} %get-tuple-element.217, ...), kind=kOutput, calls=%fused_computation.16.clone.1 | convolution fusion | flops 169492480 | bytes 2072576 | tf_op jit(solution)/shard_map/while/body/eval_jaxpr/htw,thd->wd/dot_general | solution.py:91
  73.1 2.4 %fusion.75 = f32[8,640,128]{2,1,0:T(8,128)} fusion(f32[8,640,128]{2,1,0:T(8,128)} %get-tuple-element.236, s32[]{:T(128)S(6)} %copy.74, f32[4,128]{1,0:T(4,128)S(1)} %fusion.74, f32[4,128,640]{1,2,0:T(8,128)S(1)} %get-tuple-element.216, f32[4,128]{1,0:T(4,128)S(1)} %fusion.73, f32[4,128]{1,0:T(4,128)S(1)} %get-tuple-element.217, ...), kind=kOutput, calls=%fused_computation.16.clone.1 | convolution fusion | flops 169492480 | bytes 2072576 | tf_op jit(solution)/shard_map/while/body/eval_jaxpr/htw,thd->wd/dot_general | solution.py:91
  82.2 2.4 %fusion.75 = f32[8,640,128]{2,1,0:T(8,128)} fusion(f32[8,640,128]{2,1,0:T(8,128)} %get-tuple-element.236, s32[]{:T(128)S(6)} %copy.74, f32[4,128]{1,0:T(4,128)S(1)} %fusion.74, f32[4,128,640]{1,2,0:T(8,128)S(1)} %get-tuple-element.216, f32[4,128]{1,0:T(4,128)S(1)} %fusion.73, f32[4,128]{1,0:T(4,128)S(1)} %get-tuple-element.217, ...), kind=kOutput, calls=%fused_computation.16.clone.1 | convolution fusion | flops 169492480 | bytes 2072576 | tf_op jit(solution)/shard_map/while/body/eval_jaxpr/htw,thd->wd/dot_general | solution.py:91
  91.2 2.4 %fusion.75 = f32[8,640,128]{2,1,0:T(8,128)} fusion(f32[8,640,128]{2,1,0:T(8,128)} %get-tuple-element.236, s32[]{:T(128)S(6)} %copy.74, f32[4,128]{1,0:T(4,128)S(1)} %fusion.74, f32[4,128,640]{1,2,0:T(8,128)S(1)} %get-tuple-element.216, f32[4,128]{1,0:T(4,128)S(1)} %fusion.73, f32[4,128]{1,0:T(4,128)S(1)} %get-tuple-element.217, ...), kind=kOutput, calls=%fused_computation.16.clone.1 | convolution fusion | flops 169492480 | bytes 2072576 | tf_op jit(solution)/shard_map/while/body/eval_jaxpr/htw,thd->wd/dot_general | solution.py:91
  100.3 2.3 %fusion.75 = f32[8,640,128]{2,1,0:T(8,128)} fusion(f32[8,640,128]{2,1,0:T(8,128)} %get-tuple-element.236, s32[]{:T(128)S(6)} %copy.74, f32[4,128]{1,0:T(4,128)S(1)} %fusion.74, f32[4,128,640]{1,2,0:T(8,128)S(1)} %get-tuple-element.216, f32[4,128]{1,0:T(4,128)S(1)} %fusion.73, f32[4,128]{1,0:T(4,128)S(1)} %get-tuple-element.217, ...), kind=kOutput, calls=%fused_computation.16.clone.1 | convolution fusion | flops 169492480 | bytes 2072576 | tf_op jit(solution)/shard_map/while/body/eval_jaxpr/htw,thd->wd/dot_general | solution.py:91
  109.3 2.4 %fusion.75 = f32[8,640,128]{2,1,0:T(8,128)} fusion(f32[8,640,128]{2,1,0:T(8,128)} %get-tuple-element.236, s32[]{:T(128)S(6)} %copy.74, f32[4,128]{1,0:T(4,128)S(1)} %fusion.74, f32[4,128,640]{1,2,0:T(8,128)S(1)} %get-tuple-element.216, f32[4,128]{1,0:T(4,128)S(1)} %fusion.73, f32[4,128]{1,0:T(4,128)S(1)} %get-tuple-element.217, ...), kind=kOutput, calls=%fused_computation.16.clone.1 | convolution fusion | flops 169492480 | bytes 2072576 | tf_op jit(solution)/shard_map/while/body/eval_jaxpr/htw,thd->wd/dot_general | solution.py:91
  118.3 2.4 %fusion.75 = f32[8,640,128]{2,1,0:T(8,128)} fusion(f32[8,640,128]{2,1,0:T(8,128)} %get-tuple-element.236, s32[]{:T(128)S(6)} %copy.74, f32[4,128]{1,0:T(4,128)S(1)} %fusion.74, f32[4,128,640]{1,2,0:T(8,128)S(1)} %get-tuple-element.216, f32[4,128]{1,0:T(4,128)S(1)} %fusion.73, f32[4,128]{1,0:T(4,128)S(1)} %get-tuple-element.217, ...), kind=kOutput, calls=%fused_computation.16.clone.1 | convolution fusion | flops 169492480 | bytes 2072576 | tf_op jit(solution)/shard_map/while/body/eval_jaxpr/htw,thd->wd/dot_general | solution.py:91
  122.7 3.2 %bitcast_reduce_fusion = (f32[4,640,128]{2,1,0:T(8,128)S(1)}, f32[4,640,128]{2,1,0:T(8,128)S(1)}) fusion(f32[8,640,128]{2,1,0:T(8,128)} %get-tuple-element.54, f32[8,640,128]{2,1,0:T(8,128)} %get-tuple-element.53), kind=kLoop, calls=%fused_computation.45 | loop fusion | flops 655360 | bytes 7864320 | tf_op jit(solution)/shard_map/reduce_sum | solution.py:100
  141.7 2.3 %collective-permute-done.13 = bf16[128,512]{0,1:T(8,128)(2,1)S(1)} collective-permute-done((bf16[128,512]{0,1:T(8,128)(2,1)S(1)}, bf16[128,512]{0,1:T(8,128)(2,1)S(1)}, u32[]{:S(2)}, u32[]{:S(2)}) %collective-permute-start.13) | collective-permute-done | bytes 131104 | tf_op jit(solution)/shard_map/ppermute | solution.py:20
  154.6 2.1 collective-permute-done.15
  160.2 47.5 %psum.14 = f32[]{:T(128)} all-reduce(f32[]{:T(128)S(6)} %add.96), channel_id=1, replica_groups=mesh['dp'=1,'ctx'=16,'tp'=2] {'dp','ctx','tp'}, use_global_device_ids=true, to_apply=%region_9.10 | all-reduce | flops 1 | bytes 8 | tf_op jit(solution)/shard_map/psum | solution.py:109
  208.6 5.4 %psum.15 = f32[128]{0:T(128)S(1)} all-reduce(f32[128]{0:T(128)S(1)} %add.100), channel_id=1, replica_groups=mesh['dp'=1,'ctx'=16,'tp'=2] {'tp'}, use_global_device_ids=true, to_apply=%region_12.13 | all-reduce | flops 128 | bytes 1024 | tf_op jit(solution)/shard_map/psum | solution.py:115
  (155 shorter events, 98.0 us)
Async XLA Ops:
  0.6 9.3 %copy-start.2 = (f32[1,128,512]{2,1,0:T(8,128)S(1)}, f32[1,128,512]{2,1,0:T(8,128)}, u32[]{:S(2)}) copy-start(f32[1,128,512]{2,1,0:T(8,128)} %param.13) | copy-start | bytes 786436
  0.7 22.5 %copy-start = (bf16[1,128,4096]{2,1,0:T(8,128)(2,1)S(1)}, bf16[1,128,4096]{2,1,0:T(8,128)(2,1)}, u32[]{:S(2)}) copy-start(bf16[1,128,4096]{2,1,0:T(8,128)(2,1)} %param.9) | copy-start | bytes 3145732
  0.7 11.4 %collective-permute-start = (s32[128]{0:T(128)}, s32[128]{0:T(128)S(1)}, u32[]{:S(2)}, u32[]{:S(2)}) collective-permute-start(s32[128]{0:T(128)} %bitcast.212), channel_id=1, source_target_pairs={{0,2},{2,4},{4,6},{6,8},{8,10},{10,12},{12,14},{14,16},{16,18},{18... | collective-permute-start | bytes 1544 | tf_op jit(solution)/shard_map/ppermute | solution.py:20
  5.3 25.6 %collective-permute-start.4 = (bf16[128,512]{0,1:T(8,128)(2,1)S(1)}, bf16[128,512]{0,1:T(8,128)(2,1)S(1)}, u32[]{:S(2)}, u32[]{:S(2)}) collective-permute-start(bf16[128,512]{0,1:T(8,128)(2,1)S(1)} %fusion.47), channel_id=1, source_target_pairs={{0,2},{2,4},{4,6},{6,8},{8,10},{10,12},{12,14},{14,16},{16,18},{18... | collective-permute-start | bytes 393224 | tf_op jit(solution)/shard_map/ppermute | solution.py:20
  10.1 16.6 %collective-permute-start.8 = (bf16[128,512]{0,1:T(8,128)(2,1)S(1)}, bf16[128,512]{0,1:T(8,128)(2,1)S(1)}, u32[]{:S(2)}, u32[]{:S(2)}) collective-permute-start(bf16[128,512]{0,1:T(8,128)(2,1)S(1)} %fusion.46), channel_id=1, source_target_pairs={{0,2},{2,4},{4,6},{6,8},{8,10},{10,12},{12,14},{14,16},{16,18},{18... | collective-permute-start | bytes 393224 | tf_op jit(solution)/shard_map/ppermute | solution.py:20
  12.1 4.4 %collective-permute-start.1 = (s32[128]{0:T(128)S(1)}, s32[128]{0:T(128)S(1)}, u32[]{:S(2)}, u32[]{:S(2)}) collective-permute-start(s32[128]{0:T(128)S(1)} %collective-permute-done), channel_id=1, source_target_pairs={{0,2},{2,4},{4,6},{6,8},{8,10},{10,12},{12,14},{14,16},{16,18},{18... | collective-permute-start | bytes 1544 | tf_op jit(solution)/shard_map/ppermute | solution.py:20
  16.5 3.0 %collective-permute-start.2 = (s32[128]{0:T(128)S(1)}, s32[128]{0:T(128)S(1)}, u32[]{:S(2)}, u32[]{:S(2)}) collective-permute-start(s32[128]{0:T(128)S(1)} %collective-permute-done.1), channel_id=1, source_target_pairs={{0,2},{2,4},{4,6},{6,8},{8,10},{10,12},{12,14},{14,16},{16,18},{18... | collective-permute-start | bytes 1544 | tf_op jit(solution)/shard_map/ppermute | solution.py:20
  19.5 11.4 %collective-permute-start.3 = (s32[128]{0:T(128)S(1)}, s32[128]{0:T(128)S(1)}, u32[]{:S(2)}, u32[]{:S(2)}) collective-permute-start(s32[128]{0:T(128)S(1)} %collective-permute-done.2), channel_id=1, source_target_pairs={{0,2},{2,4},{4,6},{6,8},{8,10},{10,12},{12,14},{14,16},{16,18},{18... | collective-permute-start | bytes 1544 | tf_op jit(solution)/shard_map/ppermute | solution.py:20
  25.3 19.1 %copy-start.5 = (s32[1,128]{1,0:T(1,128)S(1)}, s32[1,128]{1,0:T(1,128)}, u32[]{:S(2)}) copy-start(s32[1,128]{1,0:T(1,128)} %param.14) | copy-start | bytes 1540
  26.7 20.6 %copy-start.4 = (bf16[128,512]{0,1:T(8,128)(2,1)}, bf16[128,512]{0,1:T(8,128)(2,1)S(1)}, u32[]{:S(2)}) copy-start(bf16[128,512]{0,1:T(8,128)(2,1)S(1)} %collective-permute-done.8) | copy-start | bytes 393220
  26.7 6.4 %collective-permute-start.9 = (bf16[128,512]{0,1:T(8,128)(2,1)S(1)}, bf16[128,512]{0,1:T(8,128)(2,1)S(1)}, u32[]{:S(2)}, u32[]{:S(2)}) collective-permute-start(bf16[128,512]{0,1:T(8,128)(2,1)S(1)} %collective-permute-done.8), channel_id=1, source_target_pairs={{0,2},{2,4},{4,6},{6,8},{8,10},{10,12},{12,14},{14,16},{16,18},{18... | collective-permute-start | bytes 393224 | tf_op jit(solution)/shard_map/ppermute | solution.py:20
  30.9 7.3 %collective-permute-start.5 = (bf16[128,512]{0,1:T(8,128)(2,1)S(1)}, bf16[128,512]{0,1:T(8,128)(2,1)S(1)}, u32[]{:S(2)}, u32[]{:S(2)}) collective-permute-start(bf16[128,512]{0,1:T(8,128)(2,1)S(1)} %collective-permute-done.4), channel_id=1, source_target_pairs={{0,2},{2,4},{4,6},{6,8},{8,10},{10,12},{12,14},{14,16},{16,18},{18... | collective-permute-start | bytes 393224 | tf_op jit(solution)/shard_map/ppermute | solution.py:20
  33.1 7.0 %collective-permute-start.10 = (bf16[128,512]{0,1:T(8,128)(2,1)S(1)}, bf16[128,512]{0,1:T(8,128)(2,1)S(1)}, u32[]{:S(2)}, u32[]{:S(2)}) collective-permute-start(bf16[128,512]{0,1:T(8,128)(2,1)S(1)} %collective-permute-done.9), channel_id=1, source_target_pairs={{0,2},{2,4},{4,6},{6,8},{8,10},{10,12},{12,14},{14,16},{16,18},{18... | collective-permute-start | bytes 393224 | tf_op jit(solution)/shard_map/ppermute | solution.py:20
  38.2 6.3 %collective-permute-start.6 = (bf16[128,512]{0,1:T(8,128)(2,1)S(1)}, bf16[128,512]{0,1:T(8,128)(2,1)S(1)}, u32[]{:S(2)}, u32[]{:S(2)}) collective-permute-start(bf16[128,512]{0,1:T(8,128)(2,1)S(1)} %collective-permute-done.5), channel_id=1, source_target_pairs={{0,2},{2,4},{4,6},{6,8},{8,10},{10,12},{12,14},{14,16},{16,18},{18... | collective-permute-start | bytes 393224 | tf_op jit(solution)/shard_map/ppermute | solution.py:20
  40.1 7.2 %collective-permute-start.11 = (bf16[128,512]{0,1:T(8,128)(2,1)S(1)}, bf16[128,512]{0,1:T(8,128)(2,1)S(1)}, u32[]{:S(2)}, u32[]{:S(2)}) collective-permute-start(bf16[128,512]{0,1:T(8,128)(2,1)S(1)} %collective-permute-done.10), channel_id=1, source_target_pairs={{0,2},{2,4},{4,6},{6,8},{8,10},{10,12},{12,14},{14,16},{16,18},{18... | collective-permute-start | bytes 393224 | tf_op jit(solution)/shard_map/ppermute | solution.py:20
  44.5 3.9 %collective-permute-start.7 = (bf16[128,512]{0,1:T(8,128)(2,1)S(1)}, bf16[128,512]{0,1:T(8,128)(2,1)S(1)}, u32[]{:S(2)}, u32[]{:S(2)}) collective-permute-start(bf16[128,512]{0,1:T(8,128)(2,1)S(1)} %collective-permute-done.6), channel_id=1, source_target_pairs={{0,2},{2,4},{4,6},{6,8},{8,10},{10,12},{12,14},{14,16},{16,18},{18... | collective-permute-start | bytes 393224 | tf_op jit(solution)/shard_map/ppermute | solution.py:20
  127.1 6.0 %collective-permute-start.16 = (bf16[128,512]{0,1:T(8,128)(2,1)}, bf16[128,512]{0,1:T(8,128)(2,1)}, u32[]{:S(2)}, u32[]{:S(2)}) collective-permute-start(bf16[128,512]{0,1:T(8,128)(2,1)} %bitcast.27), channel_id=1, source_target_pairs={{2,0},{4,2},{6,4},{8,6},{10,8},{12,10},{14,12},{16,14},{18,16},{20... | collective-permute-start | bytes 393224 | tf_op jit(solution)/shard_map/ppermute | solution.py:20
  130.3 5.8 %collective-permute-start.12 = (bf16[128,512]{0,1:T(8,128)(2,1)S(1)}, bf16[128,512]{0,1:T(8,128)(2,1)}, u32[]{:S(2)}, u32[]{:S(2)}) collective-permute-start(bf16[128,512]{0,1:T(8,128)(2,1)S(1)} %bitcast.211), channel_id=1, source_target_pairs={{2,0},{4,2},{6,4},{8,6},{10,8},{12,10},{14,12},{16,14},{18,16},{20... | collective-permute-start | bytes 393224 | tf_op jit(solution)/shard_map/ppermute | solution.py:20
  134.1 6.3 %collective-permute-start.17 = (bf16[128,512]{0,1:T(8,128)(2,1)S(1)}, bf16[128,512]{0,1:T(8,128)(2,1)S(1)}, u32[]{:S(2)}, u32[]{:S(2)}) collective-permute-start(bf16[128,512]{0,1:T(8,128)(2,1)S(1)} %fusion.50), channel_id=1, source_target_pairs={{2,0},{4,2},{6,4},{8,6},{10,8},{12,10},{14,12},{16,14},{18,16},{20... | collective-permute-start | bytes 393224 | tf_op jit(solution)/shard_map/ppermute | solution.py:20
  137.0 7.0 %collective-permute-start.13 = (bf16[128,512]{0,1:T(8,128)(2,1)S(1)}, bf16[128,512]{0,1:T(8,128)(2,1)S(1)}, u32[]{:S(2)}, u32[]{:S(2)}) collective-permute-start(bf16[128,512]{0,1:T(8,128)(2,1)S(1)} %fusion.53), channel_id=1, source_target_pairs={{2,0},{4,2},{6,4},{8,6},{10,8},{12,10},{14,12},{16,14},{18,16},{20... | collective-permute-start | bytes 393224 | tf_op jit(solution)/shard_map/ppermute | solution.py:20
  140.4 7.0 %collective-permute-start.18 = (bf16[128,512]{0,1:T(8,128)(2,1)S(1)}, bf16[128,512]{0,1:T(8,128)(2,1)S(1)}, u32[]{:S(2)}, u32[]{:S(2)}) collective-permute-start(bf16[128,512]{0,1:T(8,128)(2,1)S(1)} %fusion.49), channel_id=1, source_target_pairs={{2,0},{4,2},{6,4},{8,6},{10,8},{12,10},{14,12},{16,14},{18,16},{20... | collective-permute-start | bytes 393224 | tf_op jit(solution)/shard_map/ppermute | solution.py:20
  144.1 6.3 %collective-permute-start.14 = (bf16[128,512]{0,1:T(8,128)(2,1)S(1)}, bf16[128,512]{0,1:T(8,128)(2,1)S(1)}, u32[]{:S(2)}, u32[]{:S(2)}) collective-permute-start(bf16[128,512]{0,1:T(8,128)(2,1)S(1)} %fusion.52), channel_id=1, source_target_pairs={{2,0},{4,2},{6,4},{8,6},{10,8},{12,10},{14,12},{16,14},{18,16},{20... | collective-permute-start | bytes 393224 | tf_op jit(solution)/shard_map/ppermute | solution.py:20
  147.4 6.5 %collective-permute-start.19 = (bf16[128,512]{0,1:T(8,128)(2,1)S(1)}, bf16[128,512]{0,1:T(8,128)(2,1)S(1)}, u32[]{:S(2)}, u32[]{:S(2)}) collective-permute-start(bf16[128,512]{0,1:T(8,128)(2,1)S(1)} %fusion.48), channel_id=1, source_target_pairs={{2,0},{4,2},{6,4},{8,6},{10,8},{12,10},{14,12},{16,14},{18,16},{20... | collective-permute-start | bytes 393224 | tf_op jit(solution)/shard_map/ppermute | solution.py:20
  150.4 6.3 %collective-permute-start.15 = (bf16[128,512]{0,1:T(8,128)(2,1)S(1)}, bf16[128,512]{0,1:T(8,128)(2,1)S(1)}, u32[]{:S(2)}, u32[]{:S(2)}) collective-permute-start(bf16[128,512]{0,1:T(8,128)(2,1)S(1)} %fusion.51), channel_id=1, source_target_pairs={{2,0},{4,2},{6,4},{8,6},{10,8},{12,10},{14,12},{16,14},{18,16},{20... | collective-permute-start | bytes 393224 | tf_op jit(solution)/shard_map/ppermute | solution.py:20
  (3 other events, 11.9 us)
where the time goes:
time: 217 us; the launch traced here: 216 us
  matrix products  60.5 us (28%)
  blocking collectives  52.8 us (24%)
  starting transfers between devices  49 us (23%)
  other arithmetic  19.1 us (9%)
  local copies, waits for them, and re-layouts  18.9 us (9%)
  waiting for transfers between devices  11.9 us (5%)
  between operations  3.31 us (2%)
    ppermute x20, starting transfers between devices, passed_along(): return lax.ppermute(block, axis, route)  49 us
    psum x1, blocking collectives, per_device(): overall = lax.psum(local_sq, ('dp', 'ctx', 'tp'))  47.5 us
    dot_general x8, matrix products, per_item(): jnp.einsum('htw,thd->wd', ds16, q_item, preferred_element_type=jnp.float32)  19 us
    dot_general x8, matrix products, per_item(): jnp.einsum('htw,thd->wd', prob16, t_item, preferred_element_type=jnp.floa...  15.9 us
    dot_general x8, matrix products, per_item(): jnp.einsum('htw,wd->htd', expo16, v_item, preferred_element_type=jnp.floa...  15.6 us
    ppermute x20, waiting for transfers between devices, passed_along(): return lax.ppermute(block, axis, route)  11.9 us
    dot_general x8, matrix products, per_item(): jnp.einsum('thd,wd->htw', q_item, k_item, preferred_element_type=jnp.floa...  10 us
    reduce_sum x8, other arithmetic, per_item(): jnp.sum(jnp.transpose(t_item, (1, 0, 2)).astype(jnp.float32) * out, -1, k...  7.63 us
  transfers between devices with their start and end apart: 20, of which 8 were waited for; matrix products, arithmetic and copies ran while one was open for 7% of the time, Pallas kernels for 0%

commit v1 on v0

v1 whole, which is shorter than its diff:
```python
import functools
import math

import jax
import jax.numpy as jnp
from jax import lax
from jax.experimental import pallas as pl
from jax.experimental.pallas import tpu as pltpu
from jax.sharding import PartitionSpec as P

HEADS = 64
KV_HEADS = 8
HEAD = 128
GROUP = HEADS // KV_HEADS
EXTRA = 16
LANES = 128

step_size = 0.1
radius_scale = 0.13

MESH = pl.DeviceIdType.MESH
NT = (((1,), (1,)), ((), ()))


def kernel(
    cfg,
    q_hbm, t_hbm, key_ref, value_ref, ks_ref, vs_ref, doc_ref,
    attn_hbm, nks_ref, nvs_ref,
    q_v, t_v, o_v, buf, bias, p_all, ds_all, acc, gout, gin, stat_mine, stat_in,
    load_sem, out_sem, fs_sem, fr_sem, bs_sem, br_sem, ss_sem, sr_sem,
):
    n_dp, n, n_tp, reach, kvl, tokens, tree = cfg
    total_dev = n_dp * n * n_tp
    slots = reach + 1
    width = slots * tokens
    scale = 1.0 / math.sqrt(HEAD)
    coef = scale * math.log2(math.e)
    me = lax.axis_index("ctx")
    lin = (lax.axis_index("dp") * n + me) * n_tp + lax.axis_index("tp")
    core = lax.rem(me, 2)
    xpos = lax.rem(me // 2, 2)
    mate = me + 1 - 2 * core

    def device_of(linear):
        return {
            "dp": linear // (n * n_tp),
            "ctx": lax.rem(linear // n_tp, n),
            "tp": lax.rem(linear, n_tp),
        }

    barrier = pltpu.get_barrier_semaphore()

    @pl.loop(1, total_dev)
    def _(d):
        pl.semaphore_signal(
            barrier, inc=1, device_id=device_of(lax.rem(lin + d, total_dev)), device_id_type=MESH
        )

    loads = [
        pltpu.make_async_copy(q_hbm, q_v, load_sem.at[0]),
        pltpu.make_async_copy(t_hbm, t_v, load_sem.at[1]),
    ]
    for copy in loads:
        copy.start()

    def rows_of(p):
        return pl.ds(EXTRA + p * tokens, tokens)

    def piece(p):
        return pl.ds(0, EXTRA + tokens) if p == 0 else rows_of(p)

    docs_row = doc_ref[...].astype(jnp.float32)
    buf[0, pl.ds(0, EXTRA), pl.ds(0, tokens)] = jnp.broadcast_to(docs_row, (EXTRA, tokens)).astype(
        jnp.bfloat16
    )
    buf[0, pl.ds(0, EXTRA), pl.ds(HEAD, HEAD)] = jnp.zeros((EXTRA, HEAD), jnp.bfloat16)
    for p in range(kvl):
        cols = pl.ds(p * HEAD, HEAD)
        buf[0, rows_of(p), pl.ds(0, HEAD)] = (
            key_ref[:, cols].astype(jnp.float32) + ks_ref[:, cols]
        ).astype(jnp.bfloat16)
        buf[0, rows_of(p), pl.ds(HEAD, HEAD)] = (
            value_ref[:, cols].astype(jnp.float32) + vs_ref[:, cols]
        ).astype(jnp.bfloat16)
    for k in range(1, slots):
        @pl.when(me < k)
        def _(k=k):
            buf[k] = jnp.zeros(buf.shape[1:], buf.dtype)

    has = {k: me >= k for k in range(1, slots)}

    def fsend(m, p, src, target, slot):
        return pltpu.make_async_remote_copy(
            src_ref=buf.at[src, piece(p)],
            dst_ref=buf.at[slot, piece(p)],
            send_sem=fs_sem.at[m, p],
            recv_sem=fr_sem.at[slot - 1, p],
            device_id={"ctx": target},
            device_id_type=MESH,
        )

    def frecv(slot, p):
        @pl.when(has[slot])
        def _():
            fsend(0, p, 0, me, slot).wait_recv()

    if tree:
        back_in = {
            0: (core == 0) | (me >= 3),
            1: ((core == 0) & (me >= 2)) | (me >= 5),
            2: (xpos == 0) | (me >= 4),
            3: me + 4 < n,
        }
        forward = [
            (me + 4 < n, 0, me + 4, 4),
            ((xpos == 0) | (me >= 4), 4 * xpos, me + 2 - 4 * xpos, 2),
            ((core == 0) | (me >= 2), 2 * core, mate, 1),
            (me >= 2 + 2 * core, 2 + 2 * core, mate, 3),
        ]
        backward = {
            1: (me >= 1, mate, 0),
            3: (me >= 3, mate, 1),
            2: (me >= 2, me + 2 - 4 * xpos, 2),
            4: (me >= 4, me - 4, 3),
        }
    else:
        back_in = {k - 1: me + k < n for k in range(1, slots)}
        forward = [(me + k < n, 0, me + k, k) for k in range(1, slots)]
        backward = {k: (me >= k, me - k, k - 1) for k in range(1, slots)}

    def fstart(m, p, extra=None):
        valid, src, target, slot = forward[m]
        @pl.when(valid if extra is None else valid & extra)
        def _():
            fsend(m, p, src, target, slot).start()

    for i in back_in:
        @pl.when(jnp.logical_not(back_in[i]))
        def _(i=i):
            gin[i] = jnp.zeros(gin.shape[1:], gin.dtype)

    pl.semaphore_wait(barrier, total_dev - 1)

    for p in range(kvl):
        if tree:
            fstart(0, p)
            fstart(1, p, xpos == 0)
            fstart(2, p, core == 0)
        else:
            for m in range(reach):
                fstart(m, p)

    def relay4(p):
        if tree and p < kvl:
            frecv(4, p)
            fstart(1, p, xpos == 1)

    def relay2(p):
        if tree and p < kvl:
            frecv(2, p)
            fstart(2, p, core == 1)
            fstart(3, p)

    def bsend(k, p):
        valid, target, place = backward[k]
        return pltpu.make_async_remote_copy(
            src_ref=gout.at[k - 1, p],
            dst_ref=gin.at[place, p],
            send_sem=bs_sem.at[k - 1, p],
            recv_sem=br_sem.at[place, p],
            device_id={"ctx": target},
            device_id_type=MESH,
        )

    def bstart(k, p):
        @pl.when(backward[k][0])
        def _():
            bsend(k, p).start()

    def brecv(place, p):
        @pl.when(back_in[place])
        def _():
            pltpu.make_async_remote_copy(
                src_ref=gout.at[0, p],
                dst_ref=gin.at[place, p],
                send_sem=bs_sem.at[0, p],
                recv_sem=br_sem.at[place, p],
                device_id={"ctx": me},
                device_id_type=MESH,
            ).wait_recv()

    def add(slot, place, p):
        acc[slot, p] = acc[slot, p] + gin[place, p].astype(jnp.float32)

    def step_b(p):
        if 0 <= p < kvl:
            brecv(0, p)
            brecv(1, p)
            add(2 * core, 0, p)
            add(2 + 2 * core, 1, p)
            gout[1, p] = acc[2, p].astype(jnp.bfloat16)
            bstart(2, p)

    def step_c(p):
        if 0 <= p < kvl:
            brecv(2, p)
            add(4 * xpos, 2, p)
            gout[3, p] = acc[4, p].astype(jnp.bfloat16)
            bstart(4, p)

    def step_d(p):
        if 0 <= p < kvl:
            brecv(3, p)
            add(0, 3, p)

    def make_bias():
        q_docs = docs_row
        for k in range(slots):
            k_row = docs_row if k == 0 else buf[k, pl.ds(0, EXTRA), pl.ds(0, tokens)].astype(jnp.float32)[0:1]
            k_docs = jnp.transpose(jnp.broadcast_to(k_row, (tokens, tokens)))
            ok = k_docs == q_docs
            if k == 0:
                ok = ok & (
                    lax.broadcasted_iota(jnp.int32, (tokens, tokens), 0)
                    <= lax.broadcasted_iota(jnp.int32, (tokens, tokens), 1)
                )
            off = jnp.float32(-1e38)
            shown = jnp.where(ok, jnp.float32(0.0), off)
            if k > 0:
                shown = jnp.where(me >= k, shown, off)
            bias[pl.ds(k * tokens, tokens), :] = shown

    def attend(p):
        k_all = buf[:, rows_of(p), pl.ds(0, HEAD)].reshape(width, HEAD)
        v_all = buf[:, rows_of(p), pl.ds(HEAD, HEAD)].reshape(width, HEAD)
        v_t = jnp.transpose(v_all)
        q_rows, t_rows = [], []
        for j in range(GROUP // 2):
            base = (p * GROUP + 2 * j) * HEAD
            qs = [q_v[:, pl.ds(base + i * HEAD, HEAD)] for i in range(2)]
            ts = [t_v[:, pl.ds(base + i * HEAD, HEAD)] for i in range(2)]
            q2 = jnp.concatenate(qs, 0)
            t2 = jnp.concatenate(ts, 0)
            q_rows.append(q2)
            t_rows.append(t2)
            s = lax.dot_general(k_all, q2, NT, preferred_element_type=jnp.float32)
            dp = lax.dot_general(v_all, t2, NT, preferred_element_type=jnp.float32)
            b = bias[...]
            s = s + jnp.concatenate([b, b], 1)
            top = jnp.max(s, 0, keepdims=True)
            e = jnp.exp2((s - top) * coef)
            inv = 1.0 / jnp.sum(e, 0, keepdims=True)
            delta = jnp.sum(e * dp, 0, keepdims=True) * inv
            prob = e * inv
            p16 = prob.astype(jnp.bfloat16)
            cols = pl.ds(j * 2 * tokens, 2 * tokens)
            p_all[:, cols] = p16
            ds_all[:, cols] = (prob * (dp - delta)).astype(jnp.bfloat16)
            o_t = jnp.dot(v_t, p16, preferred_element_type=jnp.float32)
            out = jnp.transpose(o_t).astype(jnp.bfloat16)
            for i in range(2):
                o_v[:, pl.ds(base + i * HEAD, HEAD)] = out[i * tokens : (i + 1) * tokens]
        q_head = jnp.concatenate(q_rows, 0)
        t_head = jnp.concatenate(t_rows, 0)
        for part, (left, right, mult) in enumerate(((ds_all, q_head, scale), (p_all, t_head, 1.0))):
            grad = jnp.dot(left[...], right, preferred_element_type=jnp.float32)
            if mult != 1.0:
                grad = grad * mult
            cols = pl.ds(part * HEAD, HEAD)
            for k in range(slots):
                block = grad[k * tokens : (k + 1) * tokens]
                if k == 0 or (tree and k % 2 == 0):
                    acc[k, p, :, cols] = block
                else:
                    gout[k - 1, p, :, cols] = block.astype(jnp.bfloat16)

    def out_copy(p):
        cols = pl.ds(p * GROUP * HEAD, GROUP * HEAD)
        return pltpu.make_async_copy(o_v.at[:, cols], attn_hbm.at[:, cols], out_sem.at[p])

    relay4(0)
    relay4(1)
    relay2(0)
    for p in range(kvl):
        relay4(p + 2)
        relay2(p + 1)
        for k in range(1, slots):
            if not (tree and k % 2 == 0):
                frecv(k, p)
        if p == 0:
            make_bias()
            for copy in loads:
                copy.wait()
        attend(p)
        out_copy(p).start()
        if tree:
            bstart(1, p)
            bstart(3, p)
            step_b(p - 1)
            step_c(p - 2)
            step_d(p - 3)
        else:
            for k in range(1, slots):
                bstart(k, p)
    if tree:
        for p in range(kvl, kvl + 3):
            step_b(p - 1)
            step_c(p - 2)
            step_d(p - 3)
    else:
        for p in range(kvl):
            for i in range(reach):
                brecv(i, p)
                add(0, i, p)

    a_sum = jnp.zeros((tokens, LANES), jnp.float32)
    b_sum = jnp.zeros((tokens, LANES), jnp.float32)
    c_sum = jnp.zeros((tokens, LANES), jnp.float32)
    for p in range(kvl):
        cols = pl.ds(p * HEAD, HEAD)
        for part, ref in enumerate((ks_ref, vs_ref)):
            old = ref[:, cols]
            g = acc[0, p, :, pl.ds(part * HEAD, HEAD)]
            a_sum += old * old
            b_sum += old * g
            c_sum += g * g
    lane = lax.broadcasted_iota(jnp.int32, (tokens, LANES), 1)
    mixed = jnp.where(
        lane == 0,
        jnp.sum(a_sum, 1, keepdims=True),
        jnp.where(
            lane == 1,
            jnp.sum(b_sum, 1, keepdims=True),
            jnp.where(lane == 2, jnp.sum(c_sum, 1, keepdims=True), 0.0),
        ),
    )
    stat_mine[...] = jnp.transpose(mixed)[0:8]

    def stat_send(d):
        return pltpu.make_async_remote_copy(
            src_ref=stat_mine,
            dst_ref=stat_in.at[d - 1],
            send_sem=ss_sem,
            recv_sem=sr_sem,
            device_id=device_of(lax.rem(lin + d, total_dev)),
            device_id_type=MESH,
        )

    @pl.loop(1, total_dev)
    def _(d):
        stat_send(d).start()

    for p in range(kvl):
        out_copy(p).wait()
        for m in range(len(forward)):
            valid, src, target, slot = forward[m]
            @pl.when(valid)
            def _(m=m, p=p, src=src, target=target, slot=slot):
                fsend(m, p, src, target, slot).wait_send()
        for k in backward:
            @pl.when(backward[k][0])
            def _(k=k, p=p):
                bsend(k, p).wait_send()

    everything = pltpu.make_async_copy(stat_in, stat_in, sr_sem)
    everything.wait()
    pltpu.make_async_copy(stat_in, stat_in, ss_sem).wait()

    mine = stat_mine[...]
    whole = mine + jnp.sum(stat_in[...], 0)
    overall = jnp.sum(whole[2:3], 1, keepdims=True)
    count = n_dp * n * tokens * 2 * KV_HEADS * HEAD
    rate = step_size / jnp.sqrt(overall / count + 1e-05)
    rows = mine
    for d in range(1, n_tp):
        tp = lax.axis_index("tp")
        peer = lin - tp + lax.rem(tp + d, n_tp)
        away = lax.rem(lin - peer + total_dev, total_dev)
        rows = rows + stat_in[away - 1]
    size_sq = jnp.maximum(rows[0:1] + 2.0 * rate * rows[1:2] + rate * rate * rows[2:3], 0.0)
    radius = radius_scale * math.sqrt(2 * KV_HEADS * HEAD)
    factor = jnp.minimum(1.0, radius / jnp.sqrt(size_sq + 1e-06))
    factor_col = jnp.transpose(jnp.broadcast_to(factor, (LANES, tokens)))
    for p in range(kvl):
        cols = pl.ds(p * HEAD, HEAD)
        nks_ref[:, cols] = (ks_ref[:, cols] + rate * acc[0, p, :, pl.ds(0, HEAD)]) * factor_col
        nvs_ref[:, cols] = (vs_ref[:, cols] + rate * acc[0, p, :, pl.ds(HEAD, HEAD)]) * factor_col


def per_device(sizes, query, key, value, key_shift, value_shift, doc_ids, target):
    n_dp, n, n_tp = sizes
    tokens = query.shape[1]
    kvl = key.shape[2] // HEAD
    channels = query.shape[2]
    seq_total = tokens * n
    doc_limit = min(2048, seq_total // 4)
    reach = (doc_limit + tokens - 2) // tokens
    slots = reach + 1
    width = slots * tokens
    tree = reach == 4 and n % 4 == 0
    places = 4 if tree else reach
    total_dev = n_dp * n * n_tp
    cfg = (n_dp, n, n_tp, reach, kvl, tokens, tree)
    bf, f32 = jnp.bfloat16, jnp.float32
    vmem = pl.BlockSpec(memory_space=pltpu.VMEM)
    anyw = pl.BlockSpec(memory_space=pl.ANY)
    dma = pltpu.SemaphoreType.DMA
    attn, nks, nvs = pl.pallas_call(
        functools.partial(kernel, cfg),
        out_shape=(
            jax.ShapeDtypeStruct((tokens, channels), bf),
            jax.ShapeDtypeStruct((tokens, kvl * HEAD), f32),
            jax.ShapeDtypeStruct((tokens, kvl * HEAD), f32),
        ),
        in_specs=[anyw, anyw, vmem, vmem, vmem, vmem, vmem],
        out_specs=(anyw, vmem, vmem),
        scratch_shapes=[
            pltpu.VMEM((tokens, channels), bf),
            pltpu.VMEM((tokens, channels), bf),
            pltpu.VMEM((tokens, channels), bf),
            pltpu.VMEM((slots, EXTRA + kvl * tokens, 2 * HEAD), bf),
            pltpu.VMEM((width, tokens), f32),
            pltpu.VMEM((width, GROUP * tokens), bf),
            pltpu.VMEM((width, GROUP * tokens), bf),
            pltpu.VMEM((slots if tree else 1, kvl, tokens, 2 * HEAD), f32),
            pltpu.VMEM((reach, kvl, tokens, 2 * HEAD), bf),
            pltpu.VMEM((places, kvl, tokens, 2 * HEAD), bf),
            pltpu.VMEM((8, LANES), f32),
            pltpu.VMEM((total_dev - 1, 8, LANES), f32),
            dma((2,)),
            dma((kvl,)),
            dma((reach, kvl)),
            dma((reach, kvl)),
            dma((reach, kvl)),
            dma((places, kvl)),
            dma,
            dma,
        ],
        compiler_params=pltpu.CompilerParams(
            collective_id=0, has_side_effects=True, vmem_limit_bytes=56 * 1024 * 1024
        ),
    )(query[0], target[0], key[0], value[0], key_shift[0], value_shift[0], doc_ids)
    return attn[None], nks[None], nvs[None]


def solution(mesh):
    sizes = (mesh.shape["dp"], mesh.shape["ctx"], mesh.shape["tp"])
    wide = P("dp", "ctx", "tp")
    return jax.shard_map(
        functools.partial(per_device, sizes),
        mesh=mesh,
        in_specs=(wide, wide, wide, wide, wide, P("dp", "ctx"), wide),
        out_specs=(wide, wide, wide),
        check_vma=False,
    )
```

time: 217 us -> 51.7 us (0.24)
  matrix products: 60.5 us -> 0 us
  blocking collectives: 52.8 us -> 0 us
  starting transfers between devices: 49 us -> 0 us
  Pallas kernels: 0 us -> 46.7 us
  other arithmetic: 19.1 us -> 0 us
  local copies, waits for them, and re-layouts: 18.9 us -> 4.08 us
  waiting for transfers between devices: 11.9 us -> 0 us
  between operations: 3.31 us -> 0.65 us
    dot_general x32 -> x0, matrix products: 60.5 us -> none  [the longest x8 19 us: per_item(): jnp.einsum('htw,thd->wd', ds16, q_item, preferred_element_type=jnp.float32)]
    psum x2 -> x0, blocking collectives: 52.8 us -> none  [the longest x1 47.5 us: per_device(): overall = lax.psum(local_sq, ('dp', 'ctx', 'tp'))]
    ppermute x20 -> x0, starting transfers between devices: 49 us -> none  [passed_along(): return lax.ppermute(block, axis, route)]
    pallas_call x0 -> x1, Pallas kernels: none -> 46.7 us  [per_device(): pl.pallas_call(functools.partial(kernel, cfg), out_shape=(jax.ShapeDtypeS...]
    reduce_sum x21 -> x0, other arithmetic: 13.9 us -> none  [the longest x8 7.63 us: per_item(): jnp.sum(jnp.transpose(t_item, (1, 0, 2)).astype(jnp.float32) * out, -1, k...]
    ppermute x20 -> x0, waiting for transfers between devices: 11.9 us -> none  [passed_along(): return lax.ppermute(block, axis, route)]
    slice x14 -> x0, local copies, waits for them, and re-layouts: 4.81 us -> none  [the longest x10 3.87 us: per_device(): carried = (moved[0] + grad_window_k[index], moved[1] + grad_window_v[index])]
    reshape x2 -> x0, local copies, waits for them, and re-layouts: 3.54 us -> none  [the longest x1 1.93 us: per_device(): out_items.reshape(kv_local, 2, half, tokens, HEAD)]
  transfers between devices with their start and end apart: 20 -> 0, of which waited for: 8 -> 0; matrix products, arithmetic and copies ran while one was open for 7% -> 0% of each run, Pallas kernels for 0% -> 0%
where the time goes in v1:
time: 51.7 us; the launch traced here: 51.5 us
  Pallas kernels  46.7 us (90%)
  local copies, waits for them, and re-layouts  4.08 us (8%)
  between operations  0.65 us (1%)
    pallas_call x1, Pallas kernels, per_device(): pl.pallas_call(functools.partial(kernel, cfg), out_shape=(jax.ShapeDtypeS...  46.7 us
    unnamed x7, local copies, waits for them, and re-layouts  4.08 us

profile of v1, /device:TPU:0, one launch (start us, length us, event | category | flops | bytes accessed | tf_op | source)
XLA Modules:
  0.0 51.5 jit_solution(13286506129951628857)
XLA Ops:
  0.6 46.7 %shard_map.94 = (bf16[128,4096]{1,0:T(8,128)(2,1)}, f32[128,512]{1,0:T(8,128)}, f32[128,512]{1,0:T(8,128)}) custom-call(bf16[128,4096]{1,0:T(8,128)(2,1)} %bitcast.9, bf16[128,4096]{1,0:T(8,128)(2,1)} %bitcast.10, bf16[128,512]{1,0:T(8,128)(2,1)} %bitcast.16, bf16[128,512]{1,0:T(8,128)(2,1)} %bitcast.17, f32[128,512]{1,0:T(8,128)} %bitcast.12, ...), custom_call_target="tpu_custom_call" | custom-call | tf_op jit(solution)/shard_map/pallas_call | solution.py:408
  47.4 0.0 copy-start.1
  47.4 2.3 %copy.13 = bf16[1,128,4096]{2,1,0:T(8,128)(2,1)} copy(bf16[1,128,4096]{2,1,0:T(8,128)(2,1)} %bitcast.11) | data formatting | bytes 2097152
  49.7 0.0 copy-done.1
  49.7 0.0 copy-start
  49.7 0.7 %copy.14 = f32[1,128,512]{2,1,0:T(8,128)} copy(f32[1,128,512]{2,1,0:T(8,128)S(1)} %bitcast.15) | data formatting | bytes 524288
  50.4 0.3 copy-done
  50.8 0.7 %copy.15 = f32[1,128,512]{2,1,0:T(8,128)} copy(f32[1,128,512]{2,1,0:T(8,128)S(1)} %bitcast.14) | data formatting | bytes 524288
Async XLA Ops:
  47.4 2.3 %copy-start.1 = (f32[128,512]{1,0:T(8,128)S(1)}, f32[128,512]{1,0:T(8,128)}, u32[]{:S(2)}) copy-start(f32[128,512]{1,0:T(8,128)} %get-tuple-element.7) | copy-start | bytes 786436
  49.7 1.0 %copy-start = (f32[128,512]{1,0:T(8,128)S(1)}, f32[128,512]{1,0:T(8,128)}, u32[]{:S(2)}) copy-start(f32[128,512]{1,0:T(8,128)} %get-tuple-element.8) | copy-start | bytes 786436

commit v2 on v1

--- a/solution.py
+++ b/solution.py
@@ -25,8 +25,8 @@
 def kernel(
     cfg,
     q_hbm, t_hbm, key_ref, value_ref, ks_ref, vs_ref, doc_ref,
-    attn_hbm, nks_ref, nvs_ref,
-    q_v, t_v, o_v, buf, bias, p_all, ds_all, acc, gout, gin, stat_mine, stat_in,
+    attn_hbm, grad_hbm, stat_ref,
+    q_v, t_v, o_v, q_t, t_t, buf, bias, acc, gout, gin, stat_mine, stat_in,
     load_sem, out_sem, fs_sem, fr_sem, bs_sem, br_sem, ss_sem, sr_sem,
 ):
     n_dp, n, n_tp, reach, kvl, tokens, tree = cfg
@@ -36,25 +36,37 @@
     scale = 1.0 / math.sqrt(HEAD)
     coef = scale * math.log2(math.e)
     me = lax.axis_index("ctx")
-    lin = (lax.axis_index("dp") * n + me) * n_tp + lax.axis_index("tp")
     core = lax.rem(me, 2)
     xpos = lax.rem(me // 2, 2)
     mate = me + 1 - 2 * core
 
-    def device_of(linear):
-        return {
-            "dp": linear // (n * n_tp),
-            "ctx": lax.rem(linear // n_tp, n),
-            "tp": lax.rem(linear, n_tp),
-        }
+    my_dp, my_tp = lax.axis_index("dp"), lax.axis_index("tp")
+
+    def wrap(index, size):
+        return jnp.where(index >= size, index - size, index)
+
+    def to_others(fn):
+        for a in range(n_dp):
+            for b in range(n_tp):
+                def one(c, a=a, b=b):
+                    place = (a * n_tp + b) * n + c
+                    fn(
+                        place - 1,
+                        {"dp": wrap(my_dp + a, n_dp), "ctx": wrap(me + c, n), "tp": wrap(my_tp + b, n_tp)},
+                    )
+                first = 1 if a == 0 and b == 0 else 0
+                if total_dev <= 64:
+                    for c in range(first, n):
+                        one(c)
+                else:
+                    pl.loop(first, n)(one)
 
     barrier = pltpu.get_barrier_semaphore()
-
-    @pl.loop(1, total_dev)
-    def _(d):
-        pl.semaphore_signal(
-            barrier, inc=1, device_id=device_of(lax.rem(lin + d, total_dev)), device_id_type=MESH
+    to_others(
+        lambda place, device: pl.semaphore_signal(
+            barrier, inc=1, device_id=device, device_id_type=MESH
         )
+    )
 
     loads = [
         pltpu.make_async_copy(q_hbm, q_v, load_sem.at[0]),
@@ -230,21 +242,34 @@
                 shown = jnp.where(me >= k, shown, off)
             bias[pl.ds(k * tokens, tokens), :] = shown
 
+    def turn(p):
+        for j in range(GROUP):
+            here = pl.ds((p * GROUP + j) * HEAD, HEAD)
+            cols = pl.ds(j * tokens, tokens)
+            q_t[p, :, cols] = jnp.transpose(q_v[:, here])
+            t_t[p, :, cols] = jnp.transpose(t_v[:, here])
+
     def attend(p):
         k_all = buf[:, rows_of(p), pl.ds(0, HEAD)].reshape(width, HEAD)
         v_all = buf[:, rows_of(p), pl.ds(HEAD, HEAD)].reshape(width, HEAD)
         v_t = jnp.transpose(v_all)
-        q_rows, t_rows = [], []
-        for j in range(GROUP // 2):
+        pairs = GROUP // 2
+
+        def products(j):
+            cols = pl.ds(j * 2 * tokens, 2 * tokens)
+            s = jnp.dot(k_all, q_t[p, :, cols], preferred_element_type=jnp.float32)
+            dp = jnp.dot(v_all, t_t[p, :, cols], preferred_element_type=jnp.float32)
+            return s, dp
+
+        grad_k = grad_v = None
+        ready = products(0)
+        for j in range(pairs):
+            s, dp = ready
+            if j + 1 < pairs:
+                ready = products(j + 1)
             base = (p * GROUP + 2 * j) * HEAD
-            qs = [q_v[:, pl.ds(base + i * HEAD, HEAD)] for i in range(2)]
-            ts = [t_v[:, pl.ds(base + i * HEAD, HEAD)] for i in range(2)]
-            q2 = jnp.concatenate(qs, 0)
-            t2 = jnp.concatenate(ts, 0)
-            q_rows.append(q2)
-            t_rows.append(t2)
-            s = lax.dot_general(k_all, q2, NT, preferred_element_type=jnp.float32)
-            dp = lax.dot_general(v_all, t2, NT, preferred_element_type=jnp.float32)
+            q2 = jnp.concatenate([q_v[:, pl.ds(base + i * HEAD, HEAD)] for i in range(2)], 0)
+            t2 = jnp.concatenate([t_v[:, pl.ds(base + i * HEAD, HEAD)] for i in range(2)], 0)
             b = bias[...]
             s = s + jnp.concatenate([b, b], 1)
             top = jnp.max(s, 0, keepdims=True)
@@ -253,19 +278,16 @@
             delta = jnp.sum(e * dp, 0, keepdims=True) * inv
             prob = e * inv
             p16 = prob.astype(jnp.bfloat16)
-            cols = pl.ds(j * 2 * tokens, 2 * tokens)
-            p_all[:, cols] = p16
-            ds_all[:, cols] = (prob * (dp - delta)).astype(jnp.bfloat16)
+            ds16 = (prob * (dp - delta)).astype(jnp.bfloat16)
             o_t = jnp.dot(v_t, p16, preferred_element_type=jnp.float32)
             out = jnp.transpose(o_t).astype(jnp.bfloat16)
             for i in range(2):
                 o_v[:, pl.ds(base + i * HEAD, HEAD)] = out[i * tokens : (i + 1) * tokens]
-        q_head = jnp.concatenate(q_rows, 0)
-        t_head = jnp.concatenate(t_rows, 0)
-        for part, (left, right, mult) in enumerate(((ds_all, q_head, scale), (p_all, t_head, 1.0))):
-            grad = jnp.dot(left[...], right, preferred_element_type=jnp.float32)
-            if mult != 1.0:
-                grad = grad * mult
+            dk = jnp.dot(ds16, q2, preferred_element_type=jnp.float32)
+            dv = jnp.dot(p16, t2, preferred_element_type=jnp.float32)
+            grad_k = dk if j == 0 else grad_k + dk
+            grad_v = dv if j == 0 else grad_v + dv
+        for part, grad in enumerate((grad_k * scale, grad_v)):
             cols = pl.ds(part * HEAD, HEAD)
             for k in range(slots):
                 block = grad[k * tokens : (k + 1) * tokens]
@@ -278,9 +300,15 @@
         cols = pl.ds(p * GROUP * HEAD, GROUP * HEAD)
         return pltpu.make_async_copy(o_v.at[:, cols], attn_hbm.at[:, cols], out_sem.at[p])
 
+    for copy in loads:
+        copy.wait()
+    turn(0)
     relay4(0)
+    turn(1)
     relay4(1)
     relay2(0)
+    for p in range(2, kvl):
+        turn(p)
     for p in range(kvl):
         relay4(p + 2)
         relay2(p + 1)
@@ -289,8 +317,6 @@
                 frecv(k, p)
         if p == 0:
             make_bias()
-            for copy in loads:
-                copy.wait()
         attend(p)
         out_copy(p).start()
         if tree:
@@ -336,19 +362,19 @@
     )
     stat_mine[...] = jnp.transpose(mixed)[0:8]
 
-    def stat_send(d):
-        return pltpu.make_async_remote_copy(
+    def stat_send(place, device):
+        pltpu.make_async_remote_copy(
             src_ref=stat_mine,
-            dst_ref=stat_in.at[d - 1],
+            dst_ref=stat_in.at[place],
             send_sem=ss_sem,
             recv_sem=sr_sem,
-            device_id=device_of(lax.rem(lin + d, total_dev)),
+            device_id=device,
             device_id_type=MESH,
-        )
-
-    @pl.loop(1, total_dev)
-    def _(d):
-        stat_send(d).start()
+        ).start()
+
+    to_others(stat_send)
+    grad_copy = pltpu.make_async_copy(acc.at[0], grad_hbm, load_sem.at[0])
+    grad_copy.start()
 
     for p in range(kvl):
         out_copy(p).wait()
@@ -372,19 +398,36 @@
     count = n_dp * n * tokens * 2 * KV_HEADS * HEAD
     rate = step_size / jnp.sqrt(overall / count + 1e-05)
     rows = mine
-    for d in range(1, n_tp):
-        tp = lax.axis_index("tp")
-        peer = lin - tp + lax.rem(tp + d, n_tp)
-        away = lax.rem(lin - peer + total_dev, total_dev)
-        rows = rows + stat_in[away - 1]
+    for b in range(1, n_tp):
+        rows = rows + stat_in[b * n - 1]
     size_sq = jnp.maximum(rows[0:1] + 2.0 * rate * rows[1:2] + rate * rate * rows[2:3], 0.0)
     radius = radius_scale * math.sqrt(2 * KV_HEADS * HEAD)
     factor = jnp.minimum(1.0, radius / jnp.sqrt(size_sq + 1e-06))
-    factor_col = jnp.transpose(jnp.broadcast_to(factor, (LANES, tokens)))
+    grad_copy.wait()
+    stat_ref[...] = jnp.where(
+        lax.broadcasted_iota(jnp.int32, (8, LANES), 0) == 0, factor, jnp.broadcast_to(rate, (8, LANES))
+    )
+
+
+def finish(kvl, tokens, attn_in, grad_ref, stat_ref, ks_ref, vs_ref, attn_out, nks_ref, nvs_ref, sem):
+    parts = 4
+    wide = attn_in.shape[1] // parts
+    copies = [
+        pltpu.make_async_copy(
+            attn_in.at[:, pl.ds(i * wide, wide)], attn_out.at[:, pl.ds(i * wide, wide)], sem.at[i]
+        )
+        for i in range(parts)
+    ]
+    for copy in copies:
+        copy.start()
+    factor = jnp.transpose(jnp.broadcast_to(stat_ref[0:1], (LANES, tokens)))
+    rate = stat_ref[1:2]
     for p in range(kvl):
         cols = pl.ds(p * HEAD, HEAD)
-        nks_ref[:, cols] = (ks_ref[:, cols] + rate * acc[0, p, :, pl.ds(0, HEAD)]) * factor_col
-        nvs_ref[:, cols] = (vs_ref[:, cols] + rate * acc[0, p, :, pl.ds(HEAD, HEAD)]) * factor_col
+        nks_ref[:, cols] = (ks_ref[:, cols] + rate * grad_ref[p, :, pl.ds(0, HEAD)]) * factor
+        nvs_ref[:, cols] = (vs_ref[:, cols] + rate * grad_ref[p, :, pl.ds(HEAD, HEAD)]) * factor
+    for copy in copies:
+        copy.wait()
 
 
 def per_device(sizes, query, key, value, key_shift, value_shift, doc_ids, target):
@@ -405,23 +448,23 @@
     vmem = pl.BlockSpec(memory_space=pltpu.VMEM)
     anyw = pl.BlockSpec(memory_space=pl.ANY)
     dma = pltpu.SemaphoreType.DMA
-    attn, nks, nvs = pl.pallas_call(
+    attn, grads, stats = pl.pallas_call(
         functools.partial(kernel, cfg),
         out_shape=(
             jax.ShapeDtypeStruct((tokens, channels), bf),
-            jax.ShapeDtypeStruct((tokens, kvl * HEAD), f32),
-            jax.ShapeDtypeStruct((tokens, kvl * HEAD), f32),
+            jax.ShapeDtypeStruct((kvl, tokens, 2 * HEAD), f32),
+            jax.ShapeDtypeStruct((8, LANES), f32),
         ),
         in_specs=[anyw, anyw, vmem, vmem, vmem, vmem, vmem],
-        out_specs=(anyw, vmem, vmem),
+        out_specs=(anyw, anyw, vmem),
         scratch_shapes=[
             pltpu.VMEM((tokens, channels), bf),
             pltpu.VMEM((tokens, channels), bf),
             pltpu.VMEM((tokens, channels), bf),
+            pltpu.VMEM((kvl, HEAD, GROUP * tokens), bf),
+            pltpu.VMEM((kvl, HEAD, GROUP * tokens), bf),
             pltpu.VMEM((slots, EXTRA + kvl * tokens, 2 * HEAD), bf),
             pltpu.VMEM((width, tokens), f32),
-            pltpu.VMEM((width, GROUP * tokens), bf),
-            pltpu.VMEM((width, GROUP * tokens), bf),
             pltpu.VMEM((slots if tree else 1, kvl, tokens, 2 * HEAD), f32),
             pltpu.VMEM((reach, kvl, tokens, 2 * HEAD), bf),
             pltpu.VMEM((places, kvl, tokens, 2 * HEAD), bf),
@@ -437,9 +480,21 @@
             dma,
         ],
         compiler_params=pltpu.CompilerParams(
-            collective_id=0, has_side_effects=True, vmem_limit_bytes=56 * 1024 * 1024
+            collective_id=0, has_side_effects=True, vmem_limit_bytes=60 * 1024 * 1024
         ),
     )(query[0], target[0], key[0], value[0], key_shift[0], value_shift[0], doc_ids)
+    attn, nks, nvs = pl.pallas_call(
+        functools.partial(finish, kvl, tokens),
+        out_shape=(
+            jax.ShapeDtypeStruct((tokens, channels), bf),
+            jax.ShapeDtypeStruct((tokens, kvl * HEAD), f32),
+            jax.ShapeDtypeStruct((tokens, kvl * HEAD), f32),
+        ),
+        in_specs=[anyw, vmem, vmem, vmem, vmem],
+        out_specs=(anyw, vmem, vmem),
+        scratch_shapes=[dma((4,))],
+        compiler_params=pltpu.CompilerParams(vmem_limit_bytes=60 * 1024 * 1024),
+    )(attn, grads, stats, key_shift[0], value_shift[0])
     return attn[None], nks[None], nvs[None]
 
 

time: 51.7 us -> 79.5 us (1.54)
  Pallas kernels: 46.7 us -> 78.7 us
  local copies, waits for them, and re-layouts: 4.08 us -> 0 us
    pallas_call x0 -> x1, Pallas kernels: none -> 34.9 us  [per_device(): pl.pallas_call(functools.partial(finish, kvl, tokens), out_shape=(jax.Sha...]
    unnamed x7 -> x0, local copies, waits for them, and re-layouts: 4.08 us -> none
    pallas_call x1, Pallas kernels: 46.7 us -> 43.8 us  [per_device(): pl.pallas_call(functools.partial(kernel, cfg), out_shape=(jax.ShapeDtypeS...]
where the time goes in v2:
time: 79.5 us; the launch traced here: 79.3 us
  Pallas kernels  78.7 us (99%)
    pallas_call x1, Pallas kernels, per_device(): pl.pallas_call(functools.partial(kernel, cfg), out_shape=(jax.ShapeDtypeS...  43.8 us
    pallas_call x1, Pallas kernels, per_device(): pl.pallas_call(functools.partial(finish, kvl, tokens), out_shape=(jax.Sha...  34.9 us

profile of v2, /device:TPU:0, one launch (start us, length us, event | category | flops | bytes accessed | tf_op | source)
XLA Modules:
  0.0 79.3 jit_solution(7937887413343456782)
XLA Ops:
  0.6 43.8 %shard_map.94 = (bf16[128,4096]{1,0:T(8,128)(2,1)}, f32[4,128,256]{2,1,0:T(8,128)}, f32[8,128]{1,0:T(8,128)}) custom-call(bf16[128,4096]{1,0:T(8,128)(2,1)} %bitcast.9, bf16[128,4096]{1,0:T(8,128)(2,1)} %bitcast.10, bf16[128,512]{1,0:T(8,128)(2,1)} %bitcast.15, bf16[128,512]{1,0:T(8,128)(2,1)} %bitcast.16, f32[128,512]{1,0:T(8,128)} %bitcast.11, ...), custom_call_target="tpu_custom_call" | custom-call | tf_op jit(solution)/shard_map/pallas_call | solution.py:451
  44.5 34.9 %shard_map.95 = (bf16[128,4096]{1,0:T(8,128)(2,1)}, f32[128,512]{1,0:T(8,128)}, f32[128,512]{1,0:T(8,128)}) custom-call(bf16[128,4096]{1,0:T(8,128)(2,1)} %get-tuple-element.9.attn_in, f32[4,128,256]{2,1,0:T(8,128)} %get-tuple-element.10.grad_ref, f32[8,128]{1,0:T(8,128)} %get-tuple-element.11.stat_ref, f32[128,512]{1,0:T(8,128)} %bitcast.12, ...), custom_call_target="tpu_custom_call" | custom-call | tf_op jit(solution)/shard_map/pallas_call | solution.py:486

commit v3 on v2

--- a/solution.py
+++ b/solution.py
@@ -24,9 +24,10 @@
 
 def kernel(
     cfg,
-    q_hbm, t_hbm, key_ref, value_ref, ks_ref, vs_ref, doc_ref,
+    q_hbm, t_hbm, key_hbm, value_hbm, ks_hbm, vs_hbm, doc_ref,
     attn_hbm, grad_hbm, stat_ref,
-    q_v, t_v, o_v, q_t, t_t, buf, bias, acc, gout, gin, stat_mine, stat_in,
+    key_ref, value_ref, ks_ref, vs_ref,
+    q_v, t_v, o_v, q_t, t_t, e_own, dp_own, row_own, buf, bias, acc, gout, gin, stat_mine, stat_in,
     load_sem, out_sem, fs_sem, fr_sem, bs_sem, br_sem, ss_sem, sr_sem,
 ):
     n_dp, n, n_tp, reach, kvl, tokens, tree = cfg
@@ -61,6 +62,14 @@
                 else:
                     pl.loop(first, n)(one)
 
+    small = [
+        pltpu.make_async_copy(src, dst, load_sem.at[2 + i])
+        for i, (src, dst) in enumerate(
+            ((key_hbm, key_ref), (ks_hbm, ks_ref), (value_hbm, value_ref), (vs_hbm, vs_ref))
+        )
+    ]
+    for copy in small:
+        copy.start()
     barrier = pltpu.get_barrier_semaphore()
     to_others(
         lambda place, device: pl.semaphore_signal(
@@ -86,6 +95,8 @@
         jnp.bfloat16
     )
     buf[0, pl.ds(0, EXTRA), pl.ds(HEAD, HEAD)] = jnp.zeros((EXTRA, HEAD), jnp.bfloat16)
+    for copy in small:
+        copy.wait()
     for p in range(kvl):
         cols = pl.ds(p * HEAD, HEAD)
         buf[0, rows_of(p), pl.ds(0, HEAD)] = (
@@ -153,7 +164,7 @@
 
     pl.semaphore_wait(barrier, total_dev - 1)
 
-    for p in range(kvl):
+    def first_sends(p):
         if tree:
             fstart(0, p)
             fstart(1, p, xpos == 0)
@@ -161,6 +172,8 @@
         else:
             for m in range(reach):
                 fstart(m, p)
+
+    first_sends(0)
 
     def relay4(p):
         if tree and p < kvl:
@@ -225,22 +238,38 @@
             brecv(3, p)
             add(0, 3, p)
 
+    off = jnp.float32(-1e38)
+
+    def own_bias():
+        ok = (jnp.transpose(jnp.broadcast_to(docs_row, (tokens, tokens))) == docs_row) & (
+            lax.broadcasted_iota(jnp.int32, (tokens, tokens), 0)
+            <= lax.broadcasted_iota(jnp.int32, (tokens, tokens), 1)
+        )
+        bias[pl.ds(0, tokens), :] = jnp.where(ok, jnp.float32(0.0), off)
+
     def make_bias():
-        q_docs = docs_row
-        for k in range(slots):
-            k_row = docs_row if k == 0 else buf[k, pl.ds(0, EXTRA), pl.ds(0, tokens)].astype(jnp.float32)[0:1]
-            k_docs = jnp.transpose(jnp.broadcast_to(k_row, (tokens, tokens)))
-            ok = k_docs == q_docs
-            if k == 0:
-                ok = ok & (
-                    lax.broadcasted_iota(jnp.int32, (tokens, tokens), 0)
-                    <= lax.broadcasted_iota(jnp.int32, (tokens, tokens), 1)
-                )
-            off = jnp.float32(-1e38)
+        for k in range(1, slots):
+            k_row = buf[k, pl.ds(0, EXTRA), pl.ds(0, tokens)].astype(jnp.float32)[0:1]
+            ok = jnp.transpose(jnp.broadcast_to(k_row, (tokens, tokens))) == docs_row
             shown = jnp.where(ok, jnp.float32(0.0), off)
-            if k > 0:
-                shown = jnp.where(me >= k, shown, off)
-            bias[pl.ds(k * tokens, tokens), :] = shown
+            bias[pl.ds(k * tokens, tokens), :] = jnp.where(me >= k, shown, off)
+
+    def own_part(p):
+        k_own = buf[0, rows_of(p), pl.ds(0, HEAD)]
+        v_own = buf[0, rows_of(p), pl.ds(HEAD, HEAD)]
+        b = bias[pl.ds(0, tokens), :]
+        b2 = jnp.concatenate([b, b], 1)
+        for j in range(GROUP // 2):
+            cols = pl.ds(j * 2 * tokens, 2 * tokens)
+            s = jnp.dot(k_own, q_t[p, :, cols], preferred_element_type=jnp.float32) + b2
+            dp = jnp.dot(v_own, t_t[p, :, cols], preferred_element_type=jnp.float32)
+            top = jnp.max(s, 0, keepdims=True)
+            e = jnp.exp2((s - top) * coef)
+            e_own[p, :, cols] = e
+            dp_own[p, :, cols] = dp
+            row_own[p, pl.ds(0, 1), cols] = top
+            row_own[p, pl.ds(1, 1), cols] = jnp.sum(e, 0, keepdims=True)
+            row_own[p, pl.ds(2, 1), cols] = jnp.sum(e * dp, 0, keepdims=True)
 
     def turn(p):
         for j in range(GROUP):
@@ -250,15 +279,16 @@
             t_t[p, :, cols] = jnp.transpose(t_v[:, here])
 
     def attend(p):
-        k_all = buf[:, rows_of(p), pl.ds(0, HEAD)].reshape(width, HEAD)
+        k_past = buf[pl.ds(1, reach), rows_of(p), pl.ds(0, HEAD)].reshape(reach * tokens, HEAD)
         v_all = buf[:, rows_of(p), pl.ds(HEAD, HEAD)].reshape(width, HEAD)
+        v_past = v_all[tokens:]
         v_t = jnp.transpose(v_all)
         pairs = GROUP // 2
 
         def products(j):
             cols = pl.ds(j * 2 * tokens, 2 * tokens)
-            s = jnp.dot(k_all, q_t[p, :, cols], preferred_element_type=jnp.float32)
-            dp = jnp.dot(v_all, t_t[p, :, cols], preferred_element_type=jnp.float32)
+            s = jnp.dot(k_past, q_t[p, :, cols], preferred_element_type=jnp.float32)
+            dp = jnp.dot(v_past, t_t[p, :, cols], preferred_element_type=jnp.float32)
             return s, dp
 
         grad_k = grad_v = None
@@ -270,15 +300,22 @@
             base = (p * GROUP + 2 * j) * HEAD
             q2 = jnp.concatenate([q_v[:, pl.ds(base + i * HEAD, HEAD)] for i in range(2)], 0)
             t2 = jnp.concatenate([t_v[:, pl.ds(base + i * HEAD, HEAD)] for i in range(2)], 0)
-            b = bias[...]
+            cols = pl.ds(j * 2 * tokens, 2 * tokens)
+            b = bias[pl.ds(tokens, reach * tokens), :]
             s = s + jnp.concatenate([b, b], 1)
-            top = jnp.max(s, 0, keepdims=True)
+            top_own = row_own[p, pl.ds(0, 1), cols]
+            top = jnp.maximum(jnp.max(s, 0, keepdims=True), top_own)
             e = jnp.exp2((s - top) * coef)
-            inv = 1.0 / jnp.sum(e, 0, keepdims=True)
-            delta = jnp.sum(e * dp, 0, keepdims=True) * inv
+            shrink = jnp.exp2((top_own - top) * coef)
+            inv = 1.0 / (jnp.sum(e, 0, keepdims=True) + row_own[p, pl.ds(1, 1), cols] * shrink)
+            delta = (
+                jnp.sum(e * dp, 0, keepdims=True) + row_own[p, pl.ds(2, 1), cols] * shrink
+            ) * inv
             prob = e * inv
-            p16 = prob.astype(jnp.bfloat16)
-            ds16 = (prob * (dp - delta)).astype(jnp.bfloat16)
+            prob_own = e_own[p, :, cols] * (shrink * inv)
+            ds_own = (prob_own * (dp_own[p, :, cols] - delta)).astype(jnp.bfloat16)
+            p16 = jnp.concatenate([prob_own.astype(jnp.bfloat16), prob.astype(jnp.bfloat16)], 0)
+            ds16 = jnp.concatenate([ds_own, (prob * (dp - delta)).astype(jnp.bfloat16)], 0)
             o_t = jnp.dot(v_t, p16, preferred_element_type=jnp.float32)
             out = jnp.transpose(o_t).astype(jnp.bfloat16)
             for i in range(2):
@@ -300,15 +337,18 @@
         cols = pl.ds(p * GROUP * HEAD, GROUP * HEAD)
         return pltpu.make_async_copy(o_v.at[:, cols], attn_hbm.at[:, cols], out_sem.at[p])
 
+    own_bias()
     for copy in loads:
         copy.wait()
-    turn(0)
-    relay4(0)
-    turn(1)
-    relay4(1)
-    relay2(0)
-    for p in range(2, kvl):
+    for p in range(kvl):
         turn(p)
+        if p + 1 < kvl:
+            first_sends(p + 1)
+        own_part(p)
+        if p < 2:
+            relay4(p)
+        if p == 1:
+            relay2(0)
     for p in range(kvl):
         relay4(p + 2)
         relay2(p + 1)
@@ -409,24 +449,42 @@
     )
 
 
-def finish(kvl, tokens, attn_in, grad_ref, stat_ref, ks_ref, vs_ref, attn_out, nks_ref, nvs_ref, sem):
+def finish(
+    kvl, tokens,
+    attn_in, grad_in, stat_ref, ks_in, vs_in, attn_out, nks_out, nvs_out,
+    held, grad_ref, ks_ref, vs_ref, nks_ref, nvs_ref, sem,
+):
     parts = 4
-    wide = attn_in.shape[1] // parts
+    high = tokens // parts
+    chunks = [pl.ds(i * high, high) for i in range(parts)]
+    fetch = [pltpu.make_async_copy(attn_in.at[c], held.at[c], sem.at[i]) for i, c in enumerate(chunks)]
     copies = [
-        pltpu.make_async_copy(
-            attn_in.at[:, pl.ds(i * wide, wide)], attn_out.at[:, pl.ds(i * wide, wide)], sem.at[i]
-        )
-        for i in range(parts)
+        pltpu.make_async_copy(held.at[c], attn_out.at[c], sem.at[parts + i])
+        for i, c in enumerate(chunks)
     ]
-    for copy in copies:
+    more = [
+        pltpu.make_async_copy(src, dst, sem.at[2 * parts + i])
+        for i, (src, dst) in enumerate(((grad_in, grad_ref), (ks_in, ks_ref), (vs_in, vs_ref)))
+    ]
+    stores = [
+        pltpu.make_async_copy(src, dst, sem.at[2 * parts + 3 + i])
+        for i, (src, dst) in enumerate(((nks_ref, nks_out), (nvs_ref, nvs_out)))
+    ]
+    for copy in fetch + more:
         copy.start()
     factor = jnp.transpose(jnp.broadcast_to(stat_ref[0:1], (LANES, tokens)))
     rate = stat_ref[1:2]
-    for p in range(kvl):
-        cols = pl.ds(p * HEAD, HEAD)
-        nks_ref[:, cols] = (ks_ref[:, cols] + rate * grad_ref[p, :, pl.ds(0, HEAD)]) * factor
-        nvs_ref[:, cols] = (vs_ref[:, cols] + rate * grad_ref[p, :, pl.ds(HEAD, HEAD)]) * factor
-    for copy in copies:
+    for i in range(parts):
+        fetch[i].wait()
+        copies[i].start()
+    for copy in more:
+        copy.wait()
+    for part, (old, new) in enumerate(((ks_ref, nks_ref), (vs_ref, nvs_ref))):
+        for p in range(kvl):
+            cols = pl.ds(p * HEAD, HEAD)
+            new[:, cols] = (old[:, cols] + rate * grad_ref[p, :, pl.ds(part * HEAD, HEAD)]) * factor
+        stores[part].start()
+    for copy in copies + stores:
         copy.wait()
 
 
@@ -455,14 +513,21 @@
             jax.ShapeDtypeStruct((kvl, tokens, 2 * HEAD), f32),
             jax.ShapeDtypeStruct((8, LANES), f32),
         ),
-        in_specs=[anyw, anyw, vmem, vmem, vmem, vmem, vmem],
+        in_specs=[anyw, anyw, anyw, anyw, anyw, anyw, vmem],
         out_specs=(anyw, anyw, vmem),
         scratch_shapes=[
+            pltpu.VMEM((tokens, kvl * HEAD), bf),
+            pltpu.VMEM((tokens, kvl * HEAD), bf),
+            pltpu.VMEM((tokens, kvl * HEAD), f32),
+            pltpu.VMEM((tokens, kvl * HEAD), f32),
             pltpu.VMEM((tokens, channels), bf),
             pltpu.VMEM((tokens, channels), bf),
             pltpu.VMEM((tokens, channels), bf),
             pltpu.VMEM((kvl, HEAD, GROUP * tokens), bf),
             pltpu.VMEM((kvl, HEAD, GROUP * tokens), bf),
+            pltpu.VMEM((kvl, tokens, GROUP * tokens), f32),
+            pltpu.VMEM((kvl, tokens, GROUP * tokens), f32),
+            pltpu.VMEM((kvl, 8, GROUP * tokens), f32),
             pltpu.VMEM((slots, EXTRA + kvl * tokens, 2 * HEAD), bf),
             pltpu.VMEM((width, tokens), f32),
             pltpu.VMEM((slots if tree else 1, kvl, tokens, 2 * HEAD), f32),
@@ -470,7 +535,7 @@
             pltpu.VMEM((places, kvl, tokens, 2 * HEAD), bf),
             pltpu.VMEM((8, LANES), f32),
             pltpu.VMEM((total_dev - 1, 8, LANES), f32),
-            dma((2,)),
+            dma((6,)),
             dma((kvl,)),
             dma((reach, kvl)),
             dma((reach, kvl)),
@@ -490,9 +555,17 @@
             jax.ShapeDtypeStruct((tokens, kvl * HEAD), f32),
             jax.ShapeDtypeStruct((tokens, kvl * HEAD), f32),
         ),
-        in_specs=[anyw, vmem, vmem, vmem, vmem],
-        out_specs=(anyw, vmem, vmem),
-        scratch_shapes=[dma((4,))],
+        in_specs=[anyw, anyw, vmem, anyw, anyw],
+        out_specs=(anyw, anyw, anyw),
+        scratch_shapes=[
+            pltpu.VMEM((tokens, channels), bf),
+            pltpu.VMEM((kvl, tokens, 2 * HEAD), f32),
+            pltpu.VMEM((tokens, kvl * HEAD), f32),
+            pltpu.VMEM((tokens, kvl * HEAD), f32),
+            pltpu.VMEM((tokens, kvl * HEAD), f32),
+            pltpu.VMEM((tokens, kvl * HEAD), f32),
+            dma((13,)),
+        ],
         compiler_params=pltpu.CompilerParams(vmem_limit_bytes=60 * 1024 * 1024),
     )(attn, grads, stats, key_shift[0], value_shift[0])
     return attn[None], nks[None], nvs[None]

time: 79.5 us -> 45.9 us (0.58)
  Pallas kernels: 78.7 us -> 45.1 us
    pallas_call x1, Pallas kernels: 34.9 us -> 3.12 us  [per_device(): pl.pallas_call(functools.partial(finish, kvl, tokens), out_shape=(jax.Sha...]
    pallas_call x1, Pallas kernels: 43.8 us -> 42 us  [per_device(): pl.pallas_call(functools.partial(kernel, cfg), out_shape=(jax.ShapeDtypeS...]
where the time goes in v3:
time: 45.9 us; the launch traced here: 45.7 us
  Pallas kernels  45.1 us (98%)
  between operations  0.64 us (1%)
    pallas_call x1, Pallas kernels, per_device(): pl.pallas_call(functools.partial(kernel, cfg), out_shape=(jax.ShapeDtypeS...  42 us
    pallas_call x1, Pallas kernels, per_device(): pl.pallas_call(functools.partial(finish, kvl, tokens), out_shape=(jax.Sha...  3.12 us

profile of v3, /device:TPU:0, one launch (start us, length us, event | category | flops | bytes accessed | tf_op | source)
XLA Modules:
  0.0 45.7 jit_solution(12727795782824392447)
XLA Ops:
  0.6 42.0 %shard_map.94 = (bf16[128,4096]{1,0:T(8,128)(2,1)}, f32[4,128,256]{2,1,0:T(8,128)}, f32[8,128]{1,0:T(8,128)}) custom-call(bf16[128,4096]{1,0:T(8,128)(2,1)} %bitcast.9, bf16[128,4096]{1,0:T(8,128)(2,1)} %bitcast.10, bf16[128,512]{1,0:T(8,128)(2,1)} %bitcast.15, bf16[128,512]{1,0:T(8,128)(2,1)} %bitcast.16, f32[128,512]{1,0:T(8,128)} %bitcast.11, ...), custom_call_target="tpu_custom_call" | custom-call | tf_op jit(solution)/shard_map/pallas_call | solution.py:509
  42.6 3.1 %shard_map.95 = (bf16[128,4096]{1,0:T(8,128)(2,1)}, f32[128,512]{1,0:T(8,128)}, f32[128,512]{1,0:T(8,128)}) custom-call(bf16[128,4096]{1,0:T(8,128)(2,1)} %get-tuple-element.9.attn_in, f32[4,128,256]{2,1,0:T(8,128)} %get-tuple-element.10.grad_in, f32[8,128]{1,0:T(8,128)} %get-tuple-element.11.stat_ref, f32[128,512]{1,0:T(8,128)} %bitcast.12, f32[128,512]{1,0:T(8,128)} %bitcast.14), custom_call_target="tpu_custom_call" | custom-call | tf_op jit(solution)/shard_map/pallas_call | solution.py:551
